TPU v7x, 32 devices: a whole 2x2x4 slice. The times are simulated.
32 devices in a mesh: seq: 8 (over y, x, core), head: 4 (over z).
Axes of the slice: x: 2, y: 2, z: 4, core: 2. Of those that a mesh axis runs over, the one named last changes fastest.
Arguments:
- queries: bfloat16 [2048, 768], P('seq', 'head'), may hold values from -9 to 9
- keys: bfloat16 [2048, 768], P('seq', 'head'), may hold values from -12 to 12
- values: bfloat16 [2048, 768], P('seq', 'head'), may hold values from -6 to 6
- out_weight: bfloat16 [768, 1536], replicated, may hold values from -0.21875 to 0.21875
- out_grad: bfloat16 [2048, 1536], P('seq', 'head'), may hold values from -6 to 6
Outputs:
- projected: bfloat16 [2048, 1536], P('seq', 'head')
- query_grad: bfloat16 [2048, 768], P('seq', 'head')
- key_grad: bfloat16 [2048, 768], P('seq', 'head')
- value_grad: bfloat16 [2048, 768], P('seq', 'head')
All inputs are finite; a program needn't handle non-finite values.
Results may differ from a plain program's by a relative error of at most 0.02.
Values may be sent and summed in bfloat16 or wider, within the bound.
A program may use at most 128 MiB of HBM per device.

v0:
```python
import math

import jax
import jax.numpy as jnp
from jax import lax
from jax.sharding import PartitionSpec as P

HD = 64


masked_score = -1e30


def contract_last(left, right):
    return lax.dot_general(
        left, right, (((1,), (1,)), ((), ())), preferred_element_type=jnp.float32
    )


def blockwise(step_fn, carried, pieces, first_row, wanted):
    count_rows = pieces[0].shape[0]
    block_rows = math.gcd(1024, count_rows)

    def one_turn(turn_index, carried_now):
        offset = turn_index * block_rows
        portions = tuple(
            (lax.dynamic_slice_in_dim(member, offset, block_rows, 0) for member in pieces)
        )
        start = first_row + offset

        def run_block(state):
            return step_fn(state, portions, start)

        def keep_state(state):
            return state

        return lax.cond(wanted(start, block_rows), run_block, keep_state, carried_now)

    return lax.fori_loop(0, count_rows // block_rows, one_turn, carried)


def per_device(queries, keys, values, out_weight, out_grad):
    local_rows = queries.shape[0]
    local_width = queries.shape[1]
    head_count = local_width // HD
    out_cols = out_grad.shape[1]
    score_scale = HD ** (-0.5)
    head_part = lax.axis_index("head")
    row_anchor = lax.axis_index("seq") * local_rows
    own_pos = row_anchor + jnp.arange(local_rows, dtype=jnp.int32)
    own_cols = lax.dynamic_slice_in_dim(out_weight, head_part * out_cols, out_cols, 1)
    query_split = queries.reshape(local_rows, head_count, HD)
    key_split = keys.reshape(local_rows, head_count, HD)
    value_split = values.reshape(local_rows, head_count, HD)

    def earlier_keys(start, count):
        return start <= row_anchor + local_rows - 1

    def later_queries(start, count):
        return start + count - 1 >= row_anchor

    partial_grad = contract_last(out_grad, own_cols)
    output_grad = lax.psum_scatter(partial_grad, "head", scatter_dimension=1, tiled=True).astype(
        jnp.bfloat16
    )
    grad_split = output_grad.reshape(local_rows, head_count, HD)

    def absorb(carried, portions, first_row):
        running_max, denominator, weighted = carried
        key_block = portions[0].reshape(-1, head_count, HD)
        value_block = portions[1].reshape(-1, head_count, HD)
        key_pos = first_row + jnp.arange(key_block.shape[0], dtype=jnp.int32)
        causal = (key_pos[None, :] <= own_pos[:, None])[:, None, :]
        scores = (
            jnp.einsum("qhc,khc->qhk", query_split, key_block, preferred_element_type=jnp.float32)
            * score_scale
        )
        scores = jnp.where(causal, scores, masked_score)
        new_max = jnp.maximum(running_max, jnp.max(scores, axis=2))
        factor = jnp.exp(running_max - new_max)
        weights = jnp.where(causal, jnp.exp(scores - new_max[:, :, None]), 0.0)
        denominator = denominator * factor + jnp.sum(weights, axis=2)
        weighted = weighted * factor[:, :, None] + jnp.einsum(
            "qhk,khc->qhc",
            weights.astype(jnp.bfloat16),
            value_block,
            preferred_element_type=jnp.float32,
        )
        return (new_max, denominator, weighted)

    start_state = (
        jnp.full((local_rows, head_count), masked_score, jnp.float32),
        jnp.zeros((local_rows, head_count), jnp.float32),
        jnp.zeros((local_rows, head_count, HD), jnp.float32),
    )
    all_keys, all_values = (
        lax.all_gather(keys, "seq", axis=0, tiled=True),
        lax.all_gather(values, "seq", axis=0, tiled=True),
    )
    running_max, denominator, weighted = blockwise(
        absorb, start_state, (all_keys, all_values), 0, earlier_keys
    )
    attended = (
        (weighted / denominator[:, :, None]).astype(jnp.bfloat16).reshape(local_rows, local_width)
    )
    log_total = running_max + jnp.log(denominator)
    projected = jnp.dot(
        lax.all_gather(attended, "head", axis=1, tiled=True),
        own_cols,
        preferred_element_type=jnp.float32,
    ).astype(jnp.bfloat16)
    row_dot = jnp.sum(
        grad_split.astype(jnp.float32)
        * attended.reshape(local_rows, head_count, HD).astype(jnp.float32),
        axis=2,
    )
    all_log, all_dot = (
        lax.all_gather(log_total.T, "seq", axis=1, tiled=True),
        lax.all_gather(row_dot.T, "seq", axis=1, tiled=True),
    )

    def query_grad_step(carried, portions, first_row):
        key_block = portions[0].reshape(-1, head_count, HD)
        value_block = portions[1].reshape(-1, head_count, HD)
        key_pos = first_row + jnp.arange(key_block.shape[0], dtype=jnp.int32)
        causal = (key_pos[None, :] <= own_pos[:, None])[:, None, :]
        scores = (
            jnp.einsum("qhc,khc->qhk", query_split, key_block, preferred_element_type=jnp.float32)
            * score_scale
        )
        scores = jnp.where(causal, scores, masked_score)
        probability = jnp.exp(scores - log_total[:, :, None])
        prob_grad = jnp.einsum(
            "qhc,khc->qhk", grad_split, value_block, preferred_element_type=jnp.float32
        )
        dscore = probability * (prob_grad - row_dot[:, :, None])
        return carried + jnp.einsum(
            "qhk,khc->qhc",
            dscore.astype(jnp.bfloat16),
            key_block,
            preferred_element_type=jnp.float32,
        )

    query_sum = blockwise(
        query_grad_step,
        jnp.zeros((local_rows, head_count, HD), jnp.float32),
        (all_keys, all_values),
        0,
        earlier_keys,
    )
    query_grad = (query_sum * score_scale).astype(jnp.bfloat16).reshape(local_rows, local_width)

    def key_grad_step(carried, portions, first_row):
        query_block = portions[0].reshape(-1, head_count, HD)
        grad_block = portions[1].reshape(-1, head_count, HD)
        block_count = query_block.shape[0]
        block_pos = first_row + jnp.arange(block_count, dtype=jnp.int32)
        causal = (own_pos[:, None] <= block_pos[None, :])[:, None, :]
        block_log = lax.dynamic_slice_in_dim(all_log, first_row, block_count, 1)
        block_dot = lax.dynamic_slice_in_dim(all_dot, first_row, block_count, 1)
        scores = (
            jnp.einsum("khc,qhc->khq", key_split, query_block, preferred_element_type=jnp.float32)
            * score_scale
        )
        scores = jnp.where(causal, scores, masked_score)
        probability = jnp.exp(scores - block_log[None, :, :])
        value_sum = carried[1] + jnp.einsum(
            "khq,qhc->khc",
            probability.astype(jnp.bfloat16),
            grad_block,
            preferred_element_type=jnp.float32,
        )
        prob_grad = jnp.einsum(
            "khc,qhc->khq", value_split, grad_block, preferred_element_type=jnp.float32
        )
        dscore = probability * (prob_grad - block_dot[None, :, :])
        key_sum = carried[0] + jnp.einsum(
            "khq,qhc->khc",
            dscore.astype(jnp.bfloat16),
            query_block,
            preferred_element_type=jnp.float32,
        )
        return (key_sum, value_sum)

    empty_grad = jnp.zeros((local_rows, head_count, HD), jnp.float32)
    key_sum, value_sum = blockwise(
        key_grad_step,
        (empty_grad, empty_grad),
        (
            lax.all_gather(queries, "seq", axis=0, tiled=True),
            lax.all_gather(output_grad, "seq", axis=0, tiled=True),
        ),
        jnp.int32(0),
        later_queries,
    )
    key_grad = (key_sum * score_scale).astype(jnp.bfloat16).reshape(local_rows, local_width)
    value_grad = value_sum.astype(jnp.bfloat16).reshape(local_rows, local_width)
    return (projected, query_grad, key_grad, value_grad)


def solution(mesh):
    return jax.shard_map(
        per_device,
        mesh=mesh,
        in_specs=(P("seq", "head"), P("seq", "head"), P("seq", "head"), P(), P("seq", "head")),
        out_specs=(P("seq", "head"), P("seq", "head"), P("seq", "head"), P("seq", "head")),
        check_vma=False,
    )
```

profile of v0, /device:TPU:1, one launch (start us, length us, event | category | flops | bytes accessed | tf_op | source)
XLA Modules:
  0.0 177.8 jit_solution(1010872927791252538)
XLA Ops:
  7.3 1.7 copy-done
  8.9 2.2 %convolution_bitcast_fusion = f32[256,768]{0,1:T(8,128)} fusion(bf16[256,384]{1,0:T(8,128)(2,1)} %param.21, bf16[768,1536]{1,0:T(8,128)(2,1)S(1)} %copy-done, s32[]{:T(128)S(6)} %select_n.72), kind=kOutput, calls=%fused_computation.66 | convolution fusion | flops 150994944 | bytes 1572868 | tf_op jit(solution)/shard_map/dot_general | solution.py:15
  11.2 1.8 copy.21
  12.9 1.7 copy.23
  14.7 14.5 %all_gather.22 = bf16[2048,192]{0,1:T(8,128)(2,1)S(1)} all-gather(bf16[256,192]{0,1:T(8,128)(2,1)S(1)} %copy-done.4), channel_id=1, replica_groups=mesh['seq'=8,'head'=4] {'seq'}, dimensions={0}, use_global_device_ids=true | all-gather | bytes 884736 | tf_op jit(solution)/shard_map/all_gather | solution.py:98
  29.1 13.3 %all_gather.21 = bf16[2048,192]{0,1:T(8,128)(2,1)} all-gather(bf16[256,192]{0,1:T(8,128)(2,1)S(1)} %copy-done.2), channel_id=1, replica_groups=mesh['seq'=8,'head'=4] {'seq'}, dimensions={0}, use_global_device_ids=true | all-gather | bytes 884736 | tf_op jit(solution)/shard_map/all_gather | solution.py:97
  43.1 5.5 %while.60 = (s32[]{:T(128)}, f32[256,3]{0,1:T(4,128)S(1)}, f32[256,3]{0,1:T(4,128)S(1)}, f32[256,3,64]{0,2,1:T(8,128)}, s32[]{:T(128)}, /*index=5*/bf16[2048,192...) while((s32[]{:T(128)}, f32[256,3]{0,1:T(4,128)S(1)}, ...), condition=%wide.region_5.6_spmd.clone, body=%wide.region_0.5_spmd.clone.sunk | while | flops 211913472 | bytes 13398333 | solution.py:39
  43.1 5.5 %conditional.10 = ((f32[256,3]{0,1:T(4,128)S(1)}, f32[256,3]{0,1:T(4,128)S(1)}, f32[256,3,64]{0,2,1:T(8,128)})) conditional(s32[]{:T(128)} %convert_element_type.127, (f32[256,3]{0,1:T(4,128)S(1)}, f32[256,3]{0,1:T(4,128)S(1)}, f32[256,3,64]{0,2,1:T(8,128)}) %tuple.201, (s32[]{:T(128)}, s32[]{:T(128)}, bf16[2048,192]{0,1:T(8,128)(2,1)}, ...), branch_computations={%region_1.1_spmd, %region_2.4_spmd} | conditional | flops 211913472 | bytes 13397070 | solution.py:37
  46.0 2.6 %fusion.15 = f32[256,3,64]{0,2,1:T(8,128)} fusion(bf16[1024,3,64]{0,2,1:T(8,128)(2,1)S(1)} %bitcast.124, f32[3,1024,256]{2,1,0:T(8,128)S(1)} %get-tuple-element.1397, f32[256,3]{0,1:T(4,128)S(1)} %max.5, pred[256,1024]{0,1:T(8,128)(4,1)S(1)} %broadcast_compare_fusion, f32[256,3,64]{0,2,1:T(8,128)} %get-tuple-element.1105, f32[256,3]{0,1:T(4,128)S(1)} %get-tuple-element.1387), kind=kOutput, calls=%fused_computation.11 | convolution fusion | flops 104693760 | bytes 4200448 | tf_op jit(solution)/shard_map/while/body/eval_jaxpr/cond/branch_1_fun/qhk,khc->qhc/dot_general | solution.py:83
  48.6 15.5 %all_gather.25 = f32[3,2048]{1,0:T(4,128)} all-gather(f32[3,256]{1,0:T(4,128)S(1)} %bitcast.140), channel_id=1, replica_groups=mesh['seq'=8,'head'=4] {'seq'}, dimensions={1}, use_global_device_ids=true | all-gather | bytes 27648 | tf_op jit(solution)/shard_map/all_gather | solution.py:118
  64.1 14.0 %all_gather.24 = bf16[2048,192]{0,1:T(8,128)(2,1)} all-gather(bf16[256,192]{0,1:T(8,128)(2,1)S(1)} %bitcast.130), channel_id=1, replica_groups=mesh['seq'=8,'head'=4] {'seq'}, dimensions={0}, use_global_device_ids=true | all-gather | bytes 884736 | tf_op jit(solution)/shard_map/all_gather | solution.py:190
  79.0 13.9 %all_gather.26 = bf16[2048,192]{0,1:T(8,128)(2,1)} all-gather(bf16[256,192]{0,1:T(8,128)(2,1)S(1)} %convert_element_type.81), channel_id=1, replica_groups=mesh['seq'=8,'head'=4] {'seq'}, dimensions={0}, use_global_device_ids=true | all-gather | bytes 884736 | tf_op jit(solution)/shard_map/all_gather | solution.py:191
  94.7 13.2 %all_gather.23 = bf16[256,768]{0,1:T(8,128)(2,1)S(1)} all-gather(bf16[256,192]{0,1:T(8,128)(2,1)S(1)} %bitcast.135), channel_id=1, replica_groups=mesh['seq'=8,'head'=4] {'head'}, dimensions={1}, use_global_device_ids=true | all-gather | bytes 491520 | tf_op jit(solution)/shard_map/all_gather | solution.py:108
  109.7 10.1 %while.61 = (s32[]{:T(128)}, f32[256,3,64]{0,2,1:T(8,128)}, s32[]{:T(128)}, bf16[2048,192]{0,1:T(8,128)(2,1)}, bf16[256,3,64]{2,1,0:T(4,128)(2,1)}, /*index=5*/f...) while((s32[]{:T(128)}, f32[256,3,64]{0,2,1:T(8,128)}, ...), condition=%wide.region_11.12_spmd.clone, body=%wide.region_8.11_spmd.clone.sunk | while | flops 307021056 | bytes 10176797 | solution.py:39
  109.7 10.1 %conditional.11 = (f32[256,3,64]{0,2,1:T(8,128)}) conditional(s32[]{:T(128)} %convert_element_type.128, f32[256,3,64]{0,2,1:T(8,128)} %get-tuple-element.1643, (s32[]{:T(128)}, s32[]{:T(128)}, bf16[2048,192]{0,1:T(8,128)(2,1)}, bf16[256,3,64]{2,1,0:T(4,128)(2,1)}, f32[256,3]{0,1:T(4,128)S(1)}, /*index=5*/bf16[2048,192]{0,1:T(8,128)(2,1)S(1)}, ...), branch_computations={%region_9.9_spmd, %region_10.10_spmd} | conditional | flops 307021056 | bytes 10175542 | solution.py:37
  109.7 1.8 %constant_dynamic-slice_fusion.2 = (bf16[1024,192]{0,1:T(8,128)(2,1)}, bf16[1024,192]{0,1:T(8,128)(2,1)S(1)}) fusion(bf16[2048,192]{0,1:T(8,128)(2,1)S(1)} %get-tuple-element.1126, s32[]{:T(128)S(6)} %select_n.66, bf16[2048,192]{0,1:T(8,128)(2,1)} %get-tuple-element.1123), kind=kLoop, calls=%fused_computation.37 | loop fusion | bytes 1572868 | tf_op jit(solution)/shard_map/while/body/eval_jaxpr/dynamic_slice | solution.py:27
  111.5 3.1 %fusion.30 = f32[3,1024,256]{1,2,0:T(8,128)} fusion(bf16[1024,3,64]{0,2,1:T(8,128)(2,1)S(1)} %bitcast.121, bf16[256,3,64]{2,1,0:T(4,128)(2,1)} %get-tuple-element.1124), kind=kOutput, calls=%fused_computation.33 | convolution fusion | flops 100663296 | bytes 3637248 | tf_op jit(solution)/shard_map/while/body/eval_jaxpr/cond/branch_1_fun/qhc,khc->qhk/dot_general | solution.py:128
  115.6 4.3 %fusion.27 = f32[256,3,64]{0,2,1:T(8,128)} fusion(f32[256,3,64]{0,2,1:T(8,128)} %get-tuple-element.1120, bf16[1024,3,64]{0,2,1:T(8,128)(2,1)S(1)} %bitcast.122, f32[3,1024,256]{1,2,0:T(8,128)} %fusion.30, bf16[1024,3,64]{0,2,1:T(8,128)(2,1)} %bitcast.127, f32[256,3]{0,1:T(4,128)S(1)} %get-tuple-element.1128, f32[256,3]{0,1:T(4,128)S(1)} %get-tuple-element.1125, ...), kind=kOutput, calls=%fused_computation.30 | convolution fusion | flops 206094336 | bytes 4691968 | tf_op jit(solution)/shard_map/while/body/eval_jaxpr/cond/branch_1_fun/qhk,khc->qhc/dot_general | solution.py:137
  119.9 1.6 multiply_convert_fusion.1
  121.5 20.6 %all_gather.27 = f32[3,2048]{1,0:T(4,128)S(1)} all-gather(f32[3,256]{1,0:T(4,128)S(1)} %bitcast.139), channel_id=1, replica_groups=mesh['seq'=8,'head'=4] {'seq'}, dimensions={1}, use_global_device_ids=true | all-gather | bytes 27648 | tf_op jit(solution)/shard_map/all_gather | solution.py:119
  143.5 24.3 %while.62 = (s32[]{:T(128)}, f32[256,3,64]{0,2,1:T(8,128)}, f32[256,3,64]{0,2,1:T(8,128)}, s32[]{:T(128)}, bf16[2048,192]{0,1:T(8,128)(2,1)}, /*index=5*/bf16[25...) while((s32[]{:T(128)}, f32[256,3,64]{0,2,1:T(8,128)}, ...), condition=%wide.region_15.16_spmd.clone.clone, body=%wide.region_12.15_spmd.clone.clone.sunk | while | flops 410879232 | bytes 14549369 | solution.py:39
  143.5 12.2 %conditional.12 = ((f32[256,3,64]{0,2,1:T(8,128)}, f32[256,3,64]{0,2,1:T(8,128)})) conditional(s32[]{:T(128)} %convert_element_type.129, (f32[256,3,64]{0,2,1:T(8,128)}, f32[256,3,64]{0,2,1:T(8,128)}) %tuple.206, (s32[]{:T(128)}, s32[]{:T(128)}, bf16[2048,192]{0,1:T(8,128)(2,1)}, bf16[256,3,64]{0,2,1:T(8,128)(2,1)}, f32[3,2048]{1,0:T(4,128)}, ...), branch_computations={%region_13.13_spmd, %region_14.14_spmd} | conditional | flops 410879232 | bytes 14548070 | solution.py:37
  143.5 1.2 constant_dynamic-slice_fusion.4
  144.6 3.2 %fusion.60 = f32[3,1024,256]{2,1,0:T(8,128)} fusion(bf16[1024,3,64]{0,2,1:T(8,128)(2,1)S(1)} %bitcast.119, bf16[256,3,64]{0,2,1:T(8,128)(2,1)} %get-tuple-element.1144), kind=kOutput, calls=%fused_computation.77 | convolution fusion | flops 100663296 | bytes 3637248 | tf_op jit(solution)/shard_map/while/body/eval_jaxpr/cond/branch_1_fun/khc,qhc->khq/dot_general | solution.py:162
  148.0 4.1 %fusion.49 = f32[256,3,64]{0,2,1:T(8,128)} fusion(f32[256,3,64]{0,2,1:T(8,128)} %get-tuple-element.1140, bf16[1024,3,64]{0,2,1:T(8,128)(2,1)S(1)} %bitcast.120, f32[3,1024,256]{2,1,0:T(8,128)} %fusion.60, bf16[1024,3,64]{0,2,1:T(8,128)(2,1)S(1)} %bitcast.125, f32[3,1024]{1,0:T(4,128)S(1)} %get-tuple-element.1395, f32[3,1024]{1,0:T(4,128)S(1)} %get-tuple-element.1394, ...), kind=kOutput, calls=%fused_computation.53 | convolution fusion | flops 206094336 | bytes 4710400 | tf_op jit(solution)/shard_map/while/body/eval_jaxpr/cond/branch_1_fun/khq,qhc->khc/dot_general | solution.py:177
  152.1 3.5 %fusion.46 = f32[256,3,64]{0,2,1:T(8,128)} fusion(f32[256,3,64]{0,2,1:T(8,128)} %get-tuple-element.1149, bf16[1024,3,64]{0,2,1:T(8,128)(2,1)S(1)} %bitcast.126, f32[3,1024,256]{2,1,0:T(8,128)} %fusion.60, f32[3,1024]{1,0:T(4,128)S(1)} %get-tuple-element.1394, pred[256,1024]{0,1:T(8,128)(4,1)S(1)} %broadcast_compare_fusion.2), kind=kOutput, calls=%fused_computation.52 | convolution fusion | flops 103858176 | bytes 4206592 | tf_op jit(solution)/shard_map/while/body/eval_jaxpr/cond/branch_1_fun/khq,qhc->khc/dot_general | solution.py:167
  155.6 12.1 %conditional.12 = ((f32[256,3,64]{0,2,1:T(8,128)}, f32[256,3,64]{0,2,1:T(8,128)})) conditional(s32[]{:T(128)} %convert_element_type.129, (f32[256,3,64]{0,2,1:T(8,128)}, f32[256,3,64]{0,2,1:T(8,128)}) %tuple.206, (s32[]{:T(128)}, s32[]{:T(128)}, bf16[2048,192]{0,1:T(8,128)(2,1)}, bf16[256,3,64]{0,2,1:T(8,128)(2,1)}, f32[3,2048]{1,0:T(4,128)}, ...), branch_computations={%region_13.13_spmd, %region_14.14_spmd} | conditional | flops 410879232 | bytes 14548070 | solution.py:37
  156.8 3.1 %fusion.60 = f32[3,1024,256]{2,1,0:T(8,128)} fusion(bf16[1024,3,64]{0,2,1:T(8,128)(2,1)S(1)} %bitcast.119, bf16[256,3,64]{0,2,1:T(8,128)(2,1)} %get-tuple-element.1144), kind=kOutput, calls=%fused_computation.77 | convolution fusion | flops 100663296 | bytes 3637248 | tf_op jit(solution)/shard_map/while/body/eval_jaxpr/cond/branch_1_fun/khc,qhc->khq/dot_general | solution.py:162
  160.2 4.1 %fusion.49 = f32[256,3,64]{0,2,1:T(8,128)} fusion(f32[256,3,64]{0,2,1:T(8,128)} %get-tuple-element.1140, bf16[1024,3,64]{0,2,1:T(8,128)(2,1)S(1)} %bitcast.120, f32[3,1024,256]{2,1,0:T(8,128)} %fusion.60, bf16[1024,3,64]{0,2,1:T(8,128)(2,1)S(1)} %bitcast.125, f32[3,1024]{1,0:T(4,128)S(1)} %get-tuple-element.1395, f32[3,1024]{1,0:T(4,128)S(1)} %get-tuple-element.1394, ...), kind=kOutput, calls=%fused_computation.53 | convolution fusion | flops 206094336 | bytes 4710400 | tf_op jit(solution)/shard_map/while/body/eval_jaxpr/cond/branch_1_fun/khq,qhc->khc/dot_general | solution.py:177
  164.3 3.5 %fusion.46 = f32[256,3,64]{0,2,1:T(8,128)} fusion(f32[256,3,64]{0,2,1:T(8,128)} %get-tuple-element.1149, bf16[1024,3,64]{0,2,1:T(8,128)(2,1)S(1)} %bitcast.126, f32[3,1024,256]{2,1,0:T(8,128)} %fusion.60, f32[3,1024]{1,0:T(4,128)S(1)} %get-tuple-element.1394, pred[256,1024]{0,1:T(8,128)(4,1)S(1)} %broadcast_compare_fusion.2), kind=kOutput, calls=%fused_computation.52 | convolution fusion | flops 103858176 | bytes 4206592 | tf_op jit(solution)/shard_map/while/body/eval_jaxpr/cond/branch_1_fun/khq,qhc->khc/dot_general | solution.py:167
  167.8 1.6 multiply_convert_fusion
  169.4 1.6 convert_element_type.86
  (54 shorter events, 12.1 us)
Async XLA Ops:
  7.2 1.8 copy-start
  7.2 35.9 %copy-start.1 = (bf16[256,192]{0,1:T(8,128)(2,1)S(1)}, bf16[256,192]{0,1:T(8,128)(2,1)}, u32[]{:S(2)}) copy-start(bf16[256,192]{0,1:T(8,128)(2,1)} %param.17) | copy-start | bytes 294916
  7.2 7.5 %copy-start.4 = (bf16[256,192]{0,1:T(8,128)(2,1)S(1)}, bf16[256,192]{0,1:T(8,128)(2,1)}, u32[]{:S(2)}) copy-start(bf16[256,192]{0,1:T(8,128)(2,1)} %param.19) | copy-start | bytes 294916
  7.2 21.9 %copy-start.2 = (bf16[256,192]{0,1:T(8,128)(2,1)S(1)}, bf16[256,192]{0,1:T(8,128)(2,1)}, u32[]{:S(2)}) copy-start(bf16[256,192]{0,1:T(8,128)(2,1)} %param.18) | copy-start | bytes 294916
  7.2 70.8 %reduce-scatter.2.cloned.1.call-start = ((), (), s32[]{:S(2)}) async-start(), calls=%async_computation.1 | async-start | bytes 983040 | tf_op jit(solution)/shard_map/reduce_scatter | solution.py:63
  143.5 4.3 %copy-start.3 = (f32[3,2048]{1,0:T(4,128)S(1)}, f32[3,2048]{1,0:T(4,128)}, u32[]{:S(2)}) copy-start(f32[3,2048]{1,0:T(4,128)} %get-tuple-element.1145) | copy-start | bytes 73732 | tf_op jit(solution)/shard_map/while/body/eval_jaxpr/cond
  155.6 4.3 %copy-start.3 = (f32[3,2048]{1,0:T(4,128)S(1)}, f32[3,2048]{1,0:T(4,128)}, u32[]{:S(2)}) copy-start(f32[3,2048]{1,0:T(4,128)} %get-tuple-element.1145) | copy-start | bytes 73732 | tf_op jit(solution)/shard_map/while/body/eval_jaxpr/cond
Sparse Core Ops, SparseCore 0:
  11.3 24.0 reduce-scatter.1
where the time goes:
time: 179 us; the launch traced here: 178 us
  blocking collectives  105 us (59%)
  matrix products  35.4 us (20%)
  local copies, waits for them, and re-layouts  14.1 us (8%)
  between operations  14.1 us (8%)
  other arithmetic  9.06 us (5%)
    all_gather x1, blocking collectives, per_device(): lax.all_gather(row_dot.T, 'seq', axis=1, tiled=True)  20.6 us
    all_gather x1, blocking collectives, per_device(): lax.all_gather(log_total.T, 'seq', axis=1, tiled=True)  15.5 us
    all_gather x1, blocking collectives, per_device(): lax.all_gather(values, 'seq', axis=0, tiled=True)  14.5 us
    all_gather x1, blocking collectives, per_device(): lax.all_gather(queries, 'seq', axis=0, tiled=True)  14 us
    all_gather x1, blocking collectives, per_device(): lax.all_gather(output_grad, 'seq', axis=0, tiled=True)  13.9 us
    all_gather x1, blocking collectives, per_device(): lax.all_gather(keys, 'seq', axis=0, tiled=True)  13.3 us
    all_gather x1, blocking collectives, per_device(): lax.all_gather(attended, 'head', axis=1, tiled=True)  13.2 us
    dot_general x2, matrix products, key_grad_step(): jnp.einsum('khq,qhc->khc', dscore.astype(jnp.bfloat16), query_block, pref...  8.16 us
  transfers between devices with their start and end apart: 1, of which 0 were waited for; matrix products, arithmetic and copies ran while one was open for 5% of the time, Pallas kernels for 0%

commit v1 on v0

v1 whole, which is shorter than its diff:
```python
import functools
import math

import jax
import jax.numpy as jnp
from jax import lax
from jax.experimental import pallas as pl
from jax.experimental.pallas import tpu as pltpu
from jax.sharding import PartitionSpec as P

HD = 64
MESH = pl.DeviceIdType.MESH
masked_score = -1e30


def round_up(value, unit):
    return -(-value // unit) * unit


def nt(left, right):
    return lax.dot_general(
        left, right, (((1,), (1,)), ((), ())), preferred_element_type=jnp.float32
    )


def nn(left, right):
    return jnp.dot(left, right, preferred_element_type=jnp.float32)


def kernel(
    n, m, q_ref, k_ref, v_ref, w_ref, og_ref,
    proj_ref, qg_ref, kg_ref, vg_ref,
    kv, qd, lr, part, got, att, wpad, qm, dom, km, vm,
    acc_a, acc_b, acc_c, max_s, sum_s, dot_s,
    w_sem, kv_send, kv_recv, qd_send, qd_recv, lr_send, lr_recv,
    pg_send, pg_recv, at_send, at_recv,
):
    rows, width = q_ref.shape
    cols = og_ref.shape[1]
    heads = width // HD
    wide = round_up(width, 128)
    pad = wide - width
    low = slice(0, wide)
    high = slice(2 * width - wide, 2 * width)
    half = rows // 2
    stat_rows = lr.shape[1]
    scale = HD ** (-0.5)
    factor = scale / math.log(2.0)
    me = lax.axis_index("seq")
    hz = lax.axis_index("head")

    def w_copy(j):
        return pltpu.make_async_copy(
            w_ref.at[pl.ds(j * width, width), pl.ds(pl.multiple_of(hz * cols, 128), cols)],
            wpad.at[j, pl.ds(pad, width), :],
            w_sem.at[j],
        )

    for j in range(m):
        w_copy(j).start()

    barrier = pltpu.get_barrier_semaphore()
    for step in range(1, m):
        other = lax.rem(hz + step, m)
        pl.semaphore_signal(barrier, inc=1, device_id=(me, other), device_id_type=MESH)

    def greet(step, carry):
        other = lax.rem(me + step, n)
        pl.semaphore_signal(barrier, inc=1, device_id=(other, hz), device_id_type=MESH)
        return carry

    lax.fori_loop(1, n, greet, 0)

    kv[me] = jnp.concatenate([k_ref[...], v_ref[...]], axis=1)
    pl.semaphore_wait(barrier, n - 1 + m - 1)

    def seq_copy(buf, send, recv, slot, dst):
        return pltpu.make_async_remote_copy(
            src_ref=buf.at[slot], dst_ref=buf.at[slot],
            send_sem=send.at[dst], recv_sem=recv.at[slot],
            device_id=(dst, hz), device_id_type=MESH,
        )

    def send_kv(j, carry):
        seq_copy(kv, kv_send, kv_recv, me, j).start()
        return carry

    lax.fori_loop(me + 1, n, send_kv, 0)

    for j in range(m):
        w_copy(j).wait()

    def share(j):
        return nt(wpad[j, pad:pad + width, :], og_ref[...])

    def part_copy(dst):
        return pltpu.make_async_remote_copy(
            src_ref=part.at[dst], dst_ref=got.at[hz],
            send_sem=pg_send.at[dst], recv_sem=pg_recv.at[hz],
            device_id=(me, dst), device_id_type=MESH,
        )

    for step in range(1, m):
        other = lax.rem(hz + step, m)
        part[other] = share(other).astype(jnp.bfloat16)
        part_copy(other).start()
    own_share = share(hz)

    lane = lax.broadcasted_iota(jnp.int32, (rows, wide), 1)

    def low_mask(h):
        return (lane >= h * HD) & (lane < (h + 1) * HD)

    def high_mask(h):
        return (lane >= pad + h * HD) & (lane < pad + (h + 1) * HD)

    q_wide = jnp.concatenate([q_ref[...], jnp.zeros((rows, pad), jnp.bfloat16)], axis=1)
    zero_16 = jnp.zeros((rows, wide), jnp.bfloat16)
    own_k = kv[me][:, low]
    own_v = kv[me][:, high]
    for h in range(heads):
        qm[h] = jnp.where(low_mask(h), q_wide, zero_16)
        km[h] = jnp.where(low_mask(h), own_k, zero_16)
        vm[h] = jnp.where(high_mask(h), own_v, zero_16)

    row_id = lax.broadcasted_iota(jnp.int32, (rows, rows), 0)
    col_id = lax.broadcasted_iota(jnp.int32, (rows, rows), 1)

    for h in range(heads):
        s = nt(qm[h], own_k) * factor
        s = jnp.where(col_id <= row_id, s, masked_score)
        top = jnp.max(s, axis=1, keepdims=True)
        e = jnp.exp2(s - top)
        max_s[h] = top
        sum_s[h] = jnp.sum(e, axis=1, keepdims=True)
        acc_a[h] = nn(e.astype(jnp.bfloat16), own_v)

    total = own_share
    for step in range(1, m):
        other = lax.rem(hz + step, m)
        pltpu.make_async_remote_copy(
            src_ref=part.at[other], dst_ref=got.at[other],
            send_sem=pg_send.at[other], recv_sem=pg_recv.at[other],
            device_id=(me, other), device_id_type=MESH,
        ).wait_recv()
        total = total + got[other].astype(jnp.float32)
    grad = total.T.astype(jnp.bfloat16)
    qd[me] = jnp.concatenate([q_ref[...], grad], axis=1)

    def send_qd(j, carry):
        seq_copy(qd, qd_send, qd_recv, me, me - 1 - j).start()
        return carry

    lax.fori_loop(0, me, send_qd, 0)
    own_g = qd[me][:, high]
    for h in range(heads):
        dom[h] = jnp.where(high_mask(h), own_g, zero_16)

    def forward(i, carry):
        j = me - 1 - i
        seq_copy(kv, kv_send, kv_recv, j, me).wait_recv()
        block = kv.at[j]
        for h in range(heads):
            s = nt(qm[h], block[:, low]) * factor
            old = max_s[h]
            top = jnp.maximum(old, jnp.max(s, axis=1, keepdims=True))
            alpha = jnp.exp2(old - top)
            e = jnp.exp2(s - top)
            max_s[h] = top
            sum_s[h] = sum_s[h] * alpha + jnp.sum(e, axis=1, keepdims=True)
            acc_a[h] = acc_a[h] * alpha + nn(e.astype(jnp.bfloat16), block[:, high])
        return carry

    lax.fori_loop(0, me, forward, 0)

    mixed = jnp.zeros((rows, wide), jnp.float32)
    for h in range(heads):
        mixed = jnp.where(high_mask(h), acc_a[h] * (1.0 / sum_s[h]), mixed)
    attended = mixed.astype(jnp.bfloat16).astype(jnp.float32)
    upper = attended[:half, pad:]
    lower = attended[half:, pad:]
    att[hz] = jnp.concatenate([upper, lower], axis=1).astype(jnp.bfloat16)

    def att_copy(slot, dst):
        return pltpu.make_async_remote_copy(
            src_ref=att.at[slot], dst_ref=att.at[slot],
            send_sem=at_send.at[dst], recv_sem=at_recv.at[slot],
            device_id=(me, dst), device_id_type=MESH,
        )

    for step in range(1, m):
        att_copy(hz, lax.rem(hz + step, m)).start()

    product = attended * own_g.astype(jnp.float32)
    stat_lane = lax.broadcasted_iota(jnp.int32, (rows, 128), 1)
    stats = jnp.zeros((rows, 128), jnp.float32)
    for h in range(heads):
        row_dot = jnp.sum(jnp.where(high_mask(h), product, 0.0), axis=1, keepdims=True)
        log_total = max_s[h] + jnp.log2(sum_s[h])
        max_s[h] = log_total
        dot_s[h] = row_dot
        stats = jnp.where(stat_lane == h, log_total, stats)
        stats = jnp.where(stat_lane == heads + h, row_dot, stats)
    lr[me] = stats.T[:stat_rows, :]

    def send_lr(j, carry):
        seq_copy(lr, lr_send, lr_recv, me, j).start()
        return carry

    lax.fori_loop(0, me, send_lr, 0)

    def query_step(block, h, own):
        s = nt(qm[h], block[:, low]) * factor
        if own:
            s = jnp.where(col_id <= row_id, s, masked_score)
        p = jnp.exp2(s - max_s[h])
        ds = p * (nt(dom[h], block[:, high]) - dot_s[h])
        return nn(ds.astype(jnp.bfloat16), block[:, low])

    for h in range(heads):
        acc_a[h] = query_step(kv.at[me], h, True)

    def query_loop(i, carry):
        block = kv.at[i]
        for h in range(heads):
            acc_a[h] = acc_a[h] + query_step(block, h, False)
        return carry

    lax.fori_loop(0, me, query_loop, 0)
    query_sum = jnp.zeros((rows, wide), jnp.float32)
    for h in range(heads):
        query_sum = jnp.where(low_mask(h), acc_a[h], query_sum)
    qg_ref[...] = (query_sum * scale).astype(jnp.bfloat16)[:, :width]

    def key_step(block, stat, h, own):
        s = nt(km[h], block[:, low]) * factor
        if own:
            s = jnp.where(row_id <= col_id, s, masked_score)
        p = jnp.exp2(s - stat[h:h + 1, :])
        value_part = nn(p.astype(jnp.bfloat16), block[:, high])
        ds = p * (nt(vm[h], block[:, high]) - stat[heads + h:heads + h + 1, :])
        return nn(ds.astype(jnp.bfloat16), block[:, low]), value_part

    for h in range(heads):
        acc_b[h], acc_c[h] = key_step(qd.at[me], lr.at[me], h, True)

    wpad[:, 0:pad, :] = jnp.zeros((m, pad, cols), jnp.bfloat16)
    wpad[:, pad + width:, :] = jnp.zeros((m, pad, cols), jnp.bfloat16)

    def project(slot):
        block = att.at[slot]
        return (
            nn(block[:, low], wpad[slot, pad:, :]),
            nn(block[:, high], wpad[slot, :wide, :]),
        )

    proj_top, proj_low = project(hz)
    for step in range(1, m):
        other = lax.rem(hz + step, m)
        att_copy(other, hz).wait_recv()
        more_top, more_low = project(other)
        proj_top = proj_top + more_top
        proj_low = proj_low + more_low
    proj_ref[:half, :] = proj_top.astype(jnp.bfloat16)
    proj_ref[half:, :] = proj_low.astype(jnp.bfloat16)

    def key_loop(j, carry):
        seq_copy(qd, qd_send, qd_recv, j, me).wait_recv()
        seq_copy(lr, lr_send, lr_recv, j, me).wait_recv()
        for h in range(heads):
            key_part, value_part = key_step(qd.at[j], lr.at[j], h, False)
            acc_b[h] = acc_b[h] + key_part
            acc_c[h] = acc_c[h] + value_part
        return carry

    lax.fori_loop(me + 1, n, key_loop, 0)
    key_sum = jnp.zeros((rows, wide), jnp.float32)
    value_sum = jnp.zeros((rows, wide), jnp.float32)
    for h in range(heads):
        key_sum = jnp.where(low_mask(h), acc_b[h], key_sum)
        value_sum = jnp.where(high_mask(h), acc_c[h], value_sum)
    kg_ref[...] = (key_sum * scale).astype(jnp.bfloat16)[:, :width]
    vg_ref[...] = value_sum[:, pad:].astype(jnp.bfloat16)

    def sent_kv(j, carry):
        seq_copy(kv, kv_send, kv_recv, me, j).wait_send()
        return carry

    lax.fori_loop(me + 1, n, sent_kv, 0)

    def sent_back(j, carry):
        seq_copy(qd, qd_send, qd_recv, me, j).wait_send()
        seq_copy(lr, lr_send, lr_recv, me, j).wait_send()
        return carry

    lax.fori_loop(0, me, sent_back, 0)
    for step in range(1, m):
        other = lax.rem(hz + step, m)
        part_copy(other).wait_send()
        att_copy(hz, other).wait_send()


def per_device(n, m, queries, keys, values, out_weight, out_grad):
    rows, width = queries.shape
    cols = out_grad.shape[1]
    heads = width // HD
    wide = round_up(width, 128)
    pad = wide - width
    stat_rows = round_up(2 * heads, 8)
    bf16, f32 = jnp.bfloat16, jnp.float32
    in_vmem = pl.BlockSpec(memory_space=pltpu.VMEM)
    dma = pltpu.SemaphoreType.DMA
    macs = rows * rows * n * 9 * width + 2 * rows * width * m * cols
    return pl.pallas_call(
        functools.partial(kernel, n, m),
        out_shape=(
            jax.ShapeDtypeStruct((rows, cols), bf16),
            jax.ShapeDtypeStruct((rows, width), bf16),
            jax.ShapeDtypeStruct((rows, width), bf16),
            jax.ShapeDtypeStruct((rows, width), bf16),
        ),
        in_specs=[in_vmem, in_vmem, in_vmem, pl.BlockSpec(memory_space=pl.ANY), in_vmem],
        out_specs=(in_vmem,) * 4,
        scratch_shapes=[
            pltpu.VMEM((n, rows, 2 * width), bf16),
            pltpu.VMEM((n, rows, 2 * width), bf16),
            pltpu.VMEM((n, stat_rows, rows), f32),
            pltpu.VMEM((m, width, rows), bf16),
            pltpu.VMEM((m, width, rows), bf16),
            pltpu.VMEM((m, rows // 2, 2 * width), bf16),
            pltpu.VMEM((m, pad + width + pad, cols), bf16),
        ]
        + [pltpu.VMEM((heads, rows, wide), bf16)] * 4
        + [pltpu.VMEM((heads, rows, wide), f32)] * 3
        + [pltpu.VMEM((heads, rows, 1), f32)] * 3
        + [dma((m,))]
        + [dma((n,))] * 6
        + [dma((m,))] * 4,
        compiler_params=pltpu.CompilerParams(
            collective_id=0, has_side_effects=True, vmem_limit_bytes=56 * 1024 * 1024
        ),
        cost_estimate=pl.CostEstimate(
            flops=macs, bytes_accessed=6 * rows * width * 2, transcendentals=rows * rows * n * heads
        ),
    )(queries, keys, values, out_weight, out_grad)


def solution(mesh):
    return jax.shard_map(
        functools.partial(per_device, mesh.shape["seq"], mesh.shape["head"]),
        mesh=mesh,
        in_specs=(P("seq", "head"), P("seq", "head"), P("seq", "head"), P(), P("seq", "head")),
        out_specs=(P("seq", "head"), P("seq", "head"), P("seq", "head"), P("seq", "head")),
        check_vma=False,
    )
```

time: 179 us -> 50.3 us (0.28)
  blocking collectives: 105 us -> 0 us
  Pallas kernels: 0 us -> 37.3 us
  matrix products: 35.4 us -> 0 us
  between operations: 14.1 us -> 0.64 us
  other arithmetic: 9.06 us -> 0 us
  local copies, waits for them, and re-layouts: 14.1 us -> 11.5 us
    all_gather x7 -> x0, blocking collectives: 105 us -> none  [the longest x1 20.6 us: per_device(): lax.all_gather(row_dot.T, 'seq', axis=1, tiled=True)]
    pallas_call x0 -> x1, Pallas kernels: none -> 37.3 us  [per_device(): pl.pallas_call(functools.partial(kernel, n, m), out_shape=(jax.ShapeDtype...]
    dot_general x12 -> x0, matrix products: 35.4 us -> none  [the longest x2 8.16 us: key_grad_step(): jnp.einsum('khq,qhc->khc', dscore.astype(jnp.bfloat16), query_block, pref...]
    convert_element_type x4 -> x0, other arithmetic: 5.67 us -> none  [the longest x1 1.58 us: per_device(): (key_sum * score_scale).astype(jnp.bfloat16)]
    dynamic_slice x6 -> x0, local copies, waits for them, and re-layouts: 5.22 us -> none  [the longest x4 5.2 us: one_turn(): lax.dynamic_slice_in_dim(member, offset, block_rows, 0)]
    pallas_call x0 -> x3, local copies, waits for them, and re-layouts: none -> 4.95 us  [per_device(): pl.pallas_call(functools.partial(kernel, n, m), out_shape=(jax.ShapeDtype...]
    another operation x4 -> x0, local copies, waits for them, and re-layouts: 2.8 us -> none
    unnamed x11 -> x4, local copies, waits for them, and re-layouts: 6.07 us -> 6.56 us
  transfers between devices with their start and end apart: 1 -> 0, of which waited for: 0 -> 0; matrix products, arithmetic and copies ran while one was open for 5% -> 0% of each run, Pallas kernels for 0% -> 0%
where the time goes in v1:
time: 50.3 us; the launch traced here: 49.4 us
  Pallas kernels  37.3 us (74%)
  local copies, waits for them, and re-layouts  11.5 us (23%)
  between operations  0.64 us (1%)
    pallas_call x1, Pallas kernels, per_device(): pl.pallas_call(functools.partial(kernel, n, m), out_shape=(jax.ShapeDtype...  37.3 us
    unnamed x4, local copies, waits for them, and re-layouts  6.56 us
    pallas_call x3, local copies, waits for them, and re-layouts, per_device(): pl.pallas_call(functools.partial(kernel, n, m), out_shape=(jax.ShapeDtype...  4.95 us

profile of v1, /device:TPU:1, one launch (start us, length us, event | category | flops | bytes accessed | tf_op | source)
XLA Modules:
  0.0 49.4 jit_solution(14947880319768581085)
XLA Ops:
  0.6 1.7 %copy.9.q_ref = bf16[256,192]{1,0:T(8,128)(2,1)} copy(bf16[256,192]{0,1:T(8,128)(2,1)} %param.5) | data formatting | bytes 196608 | tf_op args[0]
  2.3 1.6 %copy.10.k_ref = bf16[256,192]{1,0:T(8,128)(2,1)} copy(bf16[256,192]{0,1:T(8,128)(2,1)} %param.6) | data formatting | bytes 196608 | tf_op args[1]
  3.9 1.6 %copy.11.v_ref = bf16[256,192]{1,0:T(8,128)(2,1)} copy(bf16[256,192]{0,1:T(8,128)(2,1)} %param.7) | data formatting | bytes 196608 | tf_op args[2]
  5.6 37.3 %shard_map.84 = (bf16[256,384]{1,0:T(8,128)(2,1)}, bf16[256,192]{1,0:T(8,128)(2,1)}, bf16[256,192]{1,0:T(8,128)(2,1)}, bf16[256,192]{1,0:T(8,128)(2,1)}) custom-call(bf16[256,192]{1,0:T(8,128)(2,1)} %copy.9.q_ref, bf16[256,192]{1,0:T(8,128)(2,1)} %copy.10.k_ref, bf16[256,192]{1,0:T(8,128)(2,1)} %copy.11.v_ref, bf16[768,1536]{1,0:T(8,128)(2,1)} %w_ref.1, ...), custom_call_target="tpu_custom_call" | custom-call | flops 1056964608 | bytes 589824 | tf_op jit(solution)/shard_map/pallas_call | solution.py:314
  42.9 1.6 %copy.12 = bf16[256,192]{0,1:T(8,128)(2,1)} copy(bf16[256,192]{1,0:T(8,128)(2,1)} %get-tuple-element.5) | data formatting | bytes 196608 | tf_op jit(solution)/shard_map/pallas_call | solution.py:314
  44.5 1.6 %copy.13 = bf16[256,192]{0,1:T(8,128)(2,1)} copy(bf16[256,192]{1,0:T(8,128)(2,1)} %get-tuple-element.6) | data formatting | bytes 196608 | tf_op jit(solution)/shard_map/pallas_call | solution.py:314
  46.2 1.6 %copy.14 = bf16[256,192]{0,1:T(8,128)(2,1)} copy(bf16[256,192]{1,0:T(8,128)(2,1)} %get-tuple-element.7) | data formatting | bytes 196608 | tf_op jit(solution)/shard_map/pallas_call | solution.py:314
  47.8 1.6 %copy.16 = bf16[256,384]{1,0:T(8,128)(2,1)} copy(bf16[256,384]{1,0:T(8,128)(2,1)} %get-tuple-element.12) | data formatting | bytes 393216

commit v2 on v1

--- a/solution.py
+++ b/solution.py
@@ -33,9 +33,9 @@
     kv, qd, lr, part, got, att, wpad, qm, dom, km, vm,
     acc_a, acc_b, acc_c, max_s, sum_s, dot_s,
     w_sem, kv_send, kv_recv, qd_send, qd_recv, lr_send, lr_recv,
-    pg_send, pg_recv, at_send, at_recv,
+    pg_send, pg_recv, at_send, at_recv, kv_pass, qd_pass,
 ):
-    rows, width = q_ref.shape
+    width, rows = q_ref.shape
     cols = og_ref.shape[1]
     heads = width // HD
     wide = round_up(width, 128)
@@ -48,6 +48,9 @@
     factor = scale / math.log(2.0)
     me = lax.axis_index("seq")
     hz = lax.axis_index("head")
+    parity = lax.rem(me, 2)
+    pair = lax.div(me, 2)
+    sibling = 2 * pair + 1 - parity
 
     def w_copy(j):
         return pltpu.make_async_copy(
@@ -71,7 +74,7 @@
 
     lax.fori_loop(1, n, greet, 0)
 
-    kv[me] = jnp.concatenate([k_ref[...], v_ref[...]], axis=1)
+    kv[me] = jnp.concatenate([k_ref[...], v_ref[...]], axis=0).T
     pl.semaphore_wait(barrier, n - 1 + m - 1)
 
     def seq_copy(buf, send, recv, slot, dst):
@@ -81,11 +84,22 @@
             device_id=(dst, hz), device_id_type=MESH,
         )
 
-    def send_kv(j, carry):
-        seq_copy(kv, kv_send, kv_recv, me, j).start()
-        return carry
-
-    lax.fori_loop(me + 1, n, send_kv, 0)
+    def pass_on(buf, send, recv, slot):
+        return pltpu.make_async_remote_copy(
+            src_ref=buf.at[slot], dst_ref=buf.at[slot],
+            send_sem=send.at[slot], recv_sem=recv.at[slot],
+            device_id=(sibling, hz), device_id_type=MESH,
+        )
+
+    @pl.when(parity == 0)
+    def _():
+        seq_copy(kv, kv_send, kv_recv, me, sibling).start()
+
+    def send_kv(i, carry):
+        seq_copy(kv, kv_send, kv_recv, me, 2 * i + parity).start()
+        return carry
+
+    lax.fori_loop(pair + 1, n // 2, send_kv, 0)
 
     for j in range(m):
         w_copy(j).wait()
@@ -114,7 +128,7 @@
     def high_mask(h):
         return (lane >= pad + h * HD) & (lane < pad + (h + 1) * HD)
 
-    q_wide = jnp.concatenate([q_ref[...], jnp.zeros((rows, pad), jnp.bfloat16)], axis=1)
+    q_wide = jnp.concatenate([q_ref[...], jnp.zeros((pad, rows), jnp.bfloat16)], axis=0).T
     zero_16 = jnp.zeros((rows, wide), jnp.bfloat16)
     own_k = kv[me][:, low]
     own_v = kv[me][:, high]
@@ -144,21 +158,31 @@
             device_id=(me, other), device_id_type=MESH,
         ).wait_recv()
         total = total + got[other].astype(jnp.float32)
-    grad = total.T.astype(jnp.bfloat16)
-    qd[me] = jnp.concatenate([q_ref[...], grad], axis=1)
-
-    def send_qd(j, carry):
-        seq_copy(qd, qd_send, qd_recv, me, me - 1 - j).start()
-        return carry
-
-    lax.fori_loop(0, me, send_qd, 0)
+    qd[me] = jnp.concatenate([q_ref[...], total.astype(jnp.bfloat16)], axis=0).T
+
+    @pl.when(parity == 1)
+    def _():
+        seq_copy(qd, qd_send, qd_recv, me, sibling).start()
+
+    def send_qd(i, carry):
+        seq_copy(qd, qd_send, qd_recv, me, 2 * (pair - 1 - i) + parity).start()
+        return carry
+
+    lax.fori_loop(0, pair, send_qd, 0)
     own_g = qd[me][:, high]
     for h in range(heads):
         dom[h] = jnp.where(high_mask(h), own_g, zero_16)
 
     def forward(i, carry):
-        j = me - 1 - i
+        turn = i - parity + 2
+        same = (turn >= 2) & (lax.rem(turn, 2) == 0)
+        j = 2 * (pair - lax.div(turn, 2)) + jnp.where(lax.rem(turn, 2) == 0, parity, 1 - parity)
         seq_copy(kv, kv_send, kv_recv, j, me).wait_recv()
+
+        @pl.when(same)
+        def _():
+            pass_on(kv, kv_pass, kv_recv, j).start()
+
         block = kv.at[j]
         for h in range(heads):
             s = nt(qm[h], block[:, low]) * factor
@@ -230,7 +254,7 @@
     query_sum = jnp.zeros((rows, wide), jnp.float32)
     for h in range(heads):
         query_sum = jnp.where(low_mask(h), acc_a[h], query_sum)
-    qg_ref[...] = (query_sum * scale).astype(jnp.bfloat16)[:, :width]
+    qg_ref[...] = (query_sum * scale).T[:width, :].astype(jnp.bfloat16)
 
     def key_step(block, stat, h, own):
         s = nt(km[h], block[:, low]) * factor
@@ -264,8 +288,16 @@
     proj_ref[:half, :] = proj_top.astype(jnp.bfloat16)
     proj_ref[half:, :] = proj_low.astype(jnp.bfloat16)
 
-    def key_loop(j, carry):
+    def key_loop(i, carry):
+        turn = i - (1 - parity) + 2
+        same = (turn >= 2) & (lax.rem(turn, 2) == 0)
+        j = 2 * (pair + lax.div(turn, 2)) + jnp.where(lax.rem(turn, 2) == 0, parity, 1 - parity)
         seq_copy(qd, qd_send, qd_recv, j, me).wait_recv()
+
+        @pl.when(same)
+        def _():
+            pass_on(qd, qd_pass, qd_recv, j).start()
+
         seq_copy(lr, lr_send, lr_recv, j, me).wait_recv()
         for h in range(heads):
             key_part, value_part = key_step(qd.at[j], lr.at[j], h, False)
@@ -273,31 +305,52 @@
             acc_c[h] = acc_c[h] + value_part
         return carry
 
-    lax.fori_loop(me + 1, n, key_loop, 0)
+    lax.fori_loop(0, n - 1 - me, key_loop, 0)
     key_sum = jnp.zeros((rows, wide), jnp.float32)
     value_sum = jnp.zeros((rows, wide), jnp.float32)
     for h in range(heads):
         key_sum = jnp.where(low_mask(h), acc_b[h], key_sum)
         value_sum = jnp.where(high_mask(h), acc_c[h], value_sum)
-    kg_ref[...] = (key_sum * scale).astype(jnp.bfloat16)[:, :width]
-    vg_ref[...] = value_sum[:, pad:].astype(jnp.bfloat16)
-
-    def sent_kv(j, carry):
-        seq_copy(kv, kv_send, kv_recv, me, j).wait_send()
-        return carry
-
-    lax.fori_loop(me + 1, n, sent_kv, 0)
-
-    def sent_back(j, carry):
-        seq_copy(qd, qd_send, qd_recv, me, j).wait_send()
+    kg_ref[...] = (key_sum * scale).T[:width, :].astype(jnp.bfloat16)
+    vg_ref[...] = value_sum.T[pad:, :].astype(jnp.bfloat16)
+
+    @pl.when(parity == 0)
+    def _():
+        seq_copy(kv, kv_send, kv_recv, me, sibling).wait_send()
+
+    @pl.when(parity == 1)
+    def _():
+        seq_copy(qd, qd_send, qd_recv, me, sibling).wait_send()
+
+    def sent_later(i, carry):
+        seq_copy(kv, kv_send, kv_recv, me, 2 * i + parity).wait_send()
+        pass_on(qd, qd_pass, qd_recv, 2 * i + parity).wait_send()
+        return carry
+
+    lax.fori_loop(pair + 1, n // 2, sent_later, 0)
+
+    def sent_earlier(i, carry):
+        seq_copy(qd, qd_send, qd_recv, me, 2 * i + parity).wait_send()
+        pass_on(kv, kv_pass, kv_recv, 2 * i + parity).wait_send()
+        return carry
+
+    lax.fori_loop(0, pair, sent_earlier, 0)
+
+    def sent_lr(j, carry):
         seq_copy(lr, lr_send, lr_recv, me, j).wait_send()
         return carry
 
-    lax.fori_loop(0, me, sent_back, 0)
+    lax.fori_loop(0, me, sent_lr, 0)
     for step in range(1, m):
         other = lax.rem(hz + step, m)
         part_copy(other).wait_send()
         att_copy(hz, other).wait_send()
+
+
+def finish(*refs):
+    count = len(refs) // 2
+    for source, target in zip(refs[:count], refs[count:]):
+        target[...] = source[...]
 
 
 def per_device(n, m, queries, keys, values, out_weight, out_grad):
@@ -311,14 +364,15 @@
     in_vmem = pl.BlockSpec(memory_space=pltpu.VMEM)
     dma = pltpu.SemaphoreType.DMA
     macs = rows * rows * n * 9 * width + 2 * rows * width * m * cols
-    return pl.pallas_call(
+    shapes = (
+        jax.ShapeDtypeStruct((rows, cols), bf16),
+        jax.ShapeDtypeStruct((width, rows), bf16),
+        jax.ShapeDtypeStruct((width, rows), bf16),
+        jax.ShapeDtypeStruct((width, rows), bf16),
+    )
+    results = pl.pallas_call(
         functools.partial(kernel, n, m),
-        out_shape=(
-            jax.ShapeDtypeStruct((rows, cols), bf16),
-            jax.ShapeDtypeStruct((rows, width), bf16),
-            jax.ShapeDtypeStruct((rows, width), bf16),
-            jax.ShapeDtypeStruct((rows, width), bf16),
-        ),
+        out_shape=shapes,
         in_specs=[in_vmem, in_vmem, in_vmem, pl.BlockSpec(memory_space=pl.ANY), in_vmem],
         out_specs=(in_vmem,) * 4,
         scratch_shapes=[
@@ -335,14 +389,19 @@
         + [pltpu.VMEM((heads, rows, 1), f32)] * 3
         + [dma((m,))]
         + [dma((n,))] * 6
-        + [dma((m,))] * 4,
+        + [dma((m,))] * 4
+        + [dma((n,))] * 2,
         compiler_params=pltpu.CompilerParams(
             collective_id=0, has_side_effects=True, vmem_limit_bytes=56 * 1024 * 1024
         ),
         cost_estimate=pl.CostEstimate(
             flops=macs, bytes_accessed=6 * rows * width * 2, transcendentals=rows * rows * n * heads
         ),
-    )(queries, keys, values, out_weight, out_grad)
+    )(queries.T, keys.T, values.T, out_weight, out_grad)
+    projected, query_grad, key_grad, value_grad = pl.pallas_call(
+        finish, out_shape=shapes, in_specs=[in_vmem] * 4, out_specs=(in_vmem,) * 4
+    )(*results)
+    return projected, query_grad.T, key_grad.T, value_grad.T
 
 
 def solution(mesh):

time: 50.3 us -> 41.2 us (0.82)
  the two profiles are of different devices: /device:TPU:1 before, /device:TPU:30 now
where the time goes in v2:
time: 41.2 us; the launch traced here: 41.1 us
  Pallas kernels  40.4 us (98%)
  between operations  0.64 us (2%)
    pallas_call x1, Pallas kernels, per_device(): pl.pallas_call(functools.partial(kernel, n, m), out_shape=shapes, in_spec...  38.6 us
    pallas_call x1, Pallas kernels, per_device(): pl.pallas_call(finish, out_shape=shapes, in_specs=[in_vmem] * 4, out_spec...  1.86 us

profile of v2, /device:TPU:30, one launch (start us, length us, event | category | flops | bytes accessed | tf_op | source)
XLA Modules:
  0.0 41.1 jit_solution(5576841150257322218)
XLA Ops:
  0.6 38.6 %shard_map.84 = (bf16[256,384]{1,0:T(8,128)(2,1)}, bf16[192,256]{1,0:T(8,128)(2,1)}, bf16[192,256]{1,0:T(8,128)(2,1)}, bf16[192,256]{1,0:T(8,128)(2,1)}) custom-call(bf16[192,256]{1,0:T(8,128)(2,1)} %bitcast.6, bf16[192,256]{1,0:T(8,128)(2,1)} %bitcast.7, bf16[192,256]{1,0:T(8,128)(2,1)} %bitcast.8, bf16[768,1536]{1,0:T(8,128)(2,1)} %w_ref.1, ...), custom_call_target="tpu_custom_call" | custom-call | flops 1056964608 | bytes 589824 | tf_op jit(solution)/shard_map/pallas_call | solution.py:373
  39.2 1.9 %shard_map.85 = (bf16[256,384]{1,0:T(8,128)(2,1)}, bf16[192,256]{1,0:T(8,128)(2,1)}, bf16[192,256]{1,0:T(8,128)(2,1)}, bf16[192,256]{1,0:T(8,128)(2,1)}) custom-call(bf16[256,384]{1,0:T(8,128)(2,1)} %get-tuple-element.12.refs_0_, bf16[192,256]{1,0:T(8,128)(2,1)} %get-tuple-element.13.refs_1_, bf16[192,256]{1,0:T(8,128)(2,1)} %get-tuple-element.14.refs_2_, ...), custom_call_target="tpu_custom_call" | custom-call | tf_op jit(solution)/shard_map/pallas_call | solution.py:401

commit v3 on v2

--- a/solution.py
+++ b/solution.py
@@ -140,14 +140,62 @@
     row_id = lax.broadcasted_iota(jnp.int32, (rows, rows), 0)
     col_id = lax.broadcasted_iota(jnp.int32, (rows, rows), 1)
 
+    one_16 = jnp.ones((rows, wide), jnp.bfloat16)
+
+    def with_ones(block):
+        return jnp.where(lane < pad, one_16, block)
+
+    own_ones = with_ones(own_v)
     for h in range(heads):
         s = nt(qm[h], own_k) * factor
         s = jnp.where(col_id <= row_id, s, masked_score)
         top = jnp.max(s, axis=1, keepdims=True)
         e = jnp.exp2(s - top)
         max_s[h] = top
-        sum_s[h] = jnp.sum(e, axis=1, keepdims=True)
-        acc_a[h] = nn(e.astype(jnp.bfloat16), own_v)
+        acc_a[h] = nn(e.astype(jnp.bfloat16), own_ones)
+
+    def forward(i, carry):
+        turn = i - parity + 2
+        same = (turn >= 2) & (lax.rem(turn, 2) == 0)
+        j = 2 * (pair - lax.div(turn, 2)) + jnp.where(lax.rem(turn, 2) == 0, parity, 1 - parity)
+        seq_copy(kv, kv_send, kv_recv, j, me).wait_recv()
+
+        @pl.when(same)
+        def _():
+            pass_on(kv, kv_pass, kv_recv, j).start()
+
+        block = kv.at[j]
+        value_ones = with_ones(block[:, high])
+        for h in range(heads):
+            s = nt(qm[h], block[:, low]) * factor
+            old = max_s[h]
+            top = jnp.maximum(old, jnp.max(s, axis=1, keepdims=True))
+            alpha = jnp.exp2(old - top)
+            e = jnp.exp2(s - top)
+            max_s[h] = top
+            acc_a[h] = acc_a[h] * alpha + nn(e.astype(jnp.bfloat16), value_ones)
+        return carry
+
+    lax.fori_loop(0, me, forward, 0)
+
+    mixed = jnp.zeros((rows, wide), jnp.float32)
+    for h in range(heads):
+        sum_s[h] = acc_a[h][:, 0:1]
+        mixed = jnp.where(high_mask(h), acc_a[h] * (1.0 / sum_s[h]), mixed)
+    attended = mixed.astype(jnp.bfloat16).astype(jnp.float32)
+    upper = attended[:half, pad:]
+    lower = attended[half:, pad:]
+    att[hz] = jnp.concatenate([upper, lower], axis=1).astype(jnp.bfloat16)
+
+    def att_copy(slot, dst):
+        return pltpu.make_async_remote_copy(
+            src_ref=att.at[slot], dst_ref=att.at[slot],
+            send_sem=at_send.at[dst], recv_sem=at_recv.at[slot],
+            device_id=(me, dst), device_id_type=MESH,
+        )
+
+    for step in range(1, m):
+        att_copy(hz, lax.rem(hz + step, m)).start()
 
     total = own_share
     for step in range(1, m):
@@ -172,48 +220,6 @@
     own_g = qd[me][:, high]
     for h in range(heads):
         dom[h] = jnp.where(high_mask(h), own_g, zero_16)
-
-    def forward(i, carry):
-        turn = i - parity + 2
-        same = (turn >= 2) & (lax.rem(turn, 2) == 0)
-        j = 2 * (pair - lax.div(turn, 2)) + jnp.where(lax.rem(turn, 2) == 0, parity, 1 - parity)
-        seq_copy(kv, kv_send, kv_recv, j, me).wait_recv()
-
-        @pl.when(same)
-        def _():
-            pass_on(kv, kv_pass, kv_recv, j).start()
-
-        block = kv.at[j]
-        for h in range(heads):
-            s = nt(qm[h], block[:, low]) * factor
-            old = max_s[h]
-            top = jnp.maximum(old, jnp.max(s, axis=1, keepdims=True))
-            alpha = jnp.exp2(old - top)
-            e = jnp.exp2(s - top)
-            max_s[h] = top
-            sum_s[h] = sum_s[h] * alpha + jnp.sum(e, axis=1, keepdims=True)
-            acc_a[h] = acc_a[h] * alpha + nn(e.astype(jnp.bfloat16), block[:, high])
-        return carry
-
-    lax.fori_loop(0, me, forward, 0)
-
-    mixed = jnp.zeros((rows, wide), jnp.float32)
-    for h in range(heads):
-        mixed = jnp.where(high_mask(h), acc_a[h] * (1.0 / sum_s[h]), mixed)
-    attended = mixed.astype(jnp.bfloat16).astype(jnp.float32)
-    upper = attended[:half, pad:]
-    lower = attended[half:, pad:]
-    att[hz] = jnp.concatenate([upper, lower], axis=1).astype(jnp.bfloat16)
-
-    def att_copy(slot, dst):
-        return pltpu.make_async_remote_copy(
-            src_ref=att.at[slot], dst_ref=att.at[slot],
-            send_sem=at_send.at[dst], recv_sem=at_recv.at[slot],
-            device_id=(me, dst), device_id_type=MESH,
-        )
-
-    for step in range(1, m):
-        att_copy(hz, lax.rem(hz + step, m)).start()
 
     product = attended * own_g.astype(jnp.float32)
     stat_lane = lax.broadcasted_iota(jnp.int32, (rows, 128), 1)

time: 41.2 us -> 38.2 us (0.927)
  the two profiles are of different devices: /device:TPU:30 before, /device:TPU:1 now
where the time goes in v3:
time: 38.2 us; the launch traced here: 38 us
  Pallas kernels  37.4 us (98%)
  between operations  0.64 us (2%)
    pallas_call x1, Pallas kernels, per_device(): pl.pallas_call(functools.partial(kernel, n, m), out_shape=shapes, in_spec...  35.5 us
    pallas_call x1, Pallas kernels, per_device(): pl.pallas_call(finish, out_shape=shapes, in_specs=[in_vmem] * 4, out_spec...  1.86 us

profile of v3, /device:TPU:1, one launch (start us, length us, event | category | flops | bytes accessed | tf_op | source)
XLA Modules:
  0.0 38.0 jit_solution(15381890849441385270)
XLA Ops:
  0.6 35.5 %shard_map.84 = (bf16[256,384]{1,0:T(8,128)(2,1)}, bf16[192,256]{1,0:T(8,128)(2,1)}, bf16[192,256]{1,0:T(8,128)(2,1)}, bf16[192,256]{1,0:T(8,128)(2,1)}) custom-call(bf16[192,256]{1,0:T(8,128)(2,1)} %bitcast.6, bf16[192,256]{1,0:T(8,128)(2,1)} %bitcast.7, bf16[192,256]{1,0:T(8,128)(2,1)} %bitcast.8, bf16[768,1536]{1,0:T(8,128)(2,1)} %w_ref.1, ...), custom_call_target="tpu_custom_call" | custom-call | flops 1056964608 | bytes 589824 | tf_op jit(solution)/shard_map/pallas_call | solution.py:379
  36.1 1.9 %shard_map.85 = (bf16[256,384]{1,0:T(8,128)(2,1)}, bf16[192,256]{1,0:T(8,128)(2,1)}, bf16[192,256]{1,0:T(8,128)(2,1)}, bf16[192,256]{1,0:T(8,128)(2,1)}) custom-call(bf16[256,384]{1,0:T(8,128)(2,1)} %get-tuple-element.12.refs_0_, bf16[192,256]{1,0:T(8,128)(2,1)} %get-tuple-element.13.refs_1_, bf16[192,256]{1,0:T(8,128)(2,1)} %get-tuple-element.14.refs_2_, ...), custom_call_target="tpu_custom_call" | custom-call | tf_op jit(solution)/shard_map/pallas_call | solution.py:407

commit v4 on v3

--- a/solution.py
+++ b/solution.py
@@ -75,7 +75,6 @@
     lax.fori_loop(1, n, greet, 0)
 
     kv[me] = jnp.concatenate([k_ref[...], v_ref[...]], axis=0).T
-    pl.semaphore_wait(barrier, n - 1 + m - 1)
 
     def seq_copy(buf, send, recv, slot, dst):
         return pltpu.make_async_remote_copy(
@@ -91,16 +90,6 @@
             device_id=(sibling, hz), device_id_type=MESH,
         )
 
-    @pl.when(parity == 0)
-    def _():
-        seq_copy(kv, kv_send, kv_recv, me, sibling).start()
-
-    def send_kv(i, carry):
-        seq_copy(kv, kv_send, kv_recv, me, 2 * i + parity).start()
-        return carry
-
-    lax.fori_loop(pair + 1, n // 2, send_kv, 0)
-
     for j in range(m):
         w_copy(j).wait()
 
@@ -117,7 +106,20 @@
     for step in range(1, m):
         other = lax.rem(hz + step, m)
         part[other] = share(other).astype(jnp.bfloat16)
-        part_copy(other).start()
+
+    pl.semaphore_wait(barrier, n - 1 + m - 1)
+    @pl.when(parity == 0)
+    def _():
+        seq_copy(kv, kv_send, kv_recv, me, sibling).start()
+
+    def send_kv(i, carry):
+        seq_copy(kv, kv_send, kv_recv, me, 2 * i + parity).start()
+        return carry
+
+    lax.fori_loop(pair + 1, n // 2, send_kv, 0)
+
+    for step in range(1, m):
+        part_copy(lax.rem(hz + step, m)).start()
     own_share = share(hz)
 
     lane = lax.broadcasted_iota(jnp.int32, (rows, wide), 1)

time: 38.2 us -> 38.2 us (level)
  no operation moved by 1% of the time
where the time goes in v4:
time: 38.2 us; the launch traced here: 38 us
  Pallas kernels  37.3 us (98%)
  between operations  0.64 us (2%)
    pallas_call x1, Pallas kernels, per_device(): pl.pallas_call(functools.partial(kernel, n, m), out_shape=shapes, in_spec...  35.5 us
    pallas_call x1, Pallas kernels, per_device(): pl.pallas_call(finish, out_shape=shapes, in_specs=[in_vmem] * 4, out_spec...  1.86 us

profile of v4, /device:TPU:1, one launch (start us, length us, event | category | flops | bytes accessed | tf_op | source)
XLA Modules:
  0.0 38.0 jit_solution(3370932819371201621)
XLA Ops:
  0.6 35.5 %shard_map.84 = (bf16[256,384]{1,0:T(8,128)(2,1)}, bf16[192,256]{1,0:T(8,128)(2,1)}, bf16[192,256]{1,0:T(8,128)(2,1)}, bf16[192,256]{1,0:T(8,128)(2,1)}) custom-call(bf16[192,256]{1,0:T(8,128)(2,1)} %bitcast.6, bf16[192,256]{1,0:T(8,128)(2,1)} %bitcast.7, bf16[192,256]{1,0:T(8,128)(2,1)} %bitcast.8, bf16[768,1536]{1,0:T(8,128)(2,1)} %w_ref.1, ...), custom_call_target="tpu_custom_call" | custom-call | flops 1056964608 | bytes 589824 | tf_op jit(solution)/shard_map/pallas_call | solution.py:381
  36.1 1.9 %shard_map.85 = (bf16[256,384]{1,0:T(8,128)(2,1)}, bf16[192,256]{1,0:T(8,128)(2,1)}, bf16[192,256]{1,0:T(8,128)(2,1)}, bf16[192,256]{1,0:T(8,128)(2,1)}) custom-call(bf16[256,384]{1,0:T(8,128)(2,1)} %get-tuple-element.12.refs_0_, bf16[192,256]{1,0:T(8,128)(2,1)} %get-tuple-element.13.refs_1_, bf16[192,256]{1,0:T(8,128)(2,1)} %get-tuple-element.14.refs_2_, ...), custom_call_target="tpu_custom_call" | custom-call | tf_op jit(solution)/shard_map/pallas_call | solution.py:409

commit v5 on v3

--- a/solution.py
+++ b/solution.py
@@ -31,7 +31,7 @@
     n, m, q_ref, k_ref, v_ref, w_ref, og_ref,
     proj_ref, qg_ref, kg_ref, vg_ref,
     kv, qd, lr, part, got, att, wpad, qm, dom, km, vm,
-    acc_a, acc_b, acc_c, max_s, sum_s, dot_s,
+    acc_a, acc_b, acc_c, max_s, dot_s, acc_t, max_r, sum_r,
     w_sem, kv_send, kv_recv, qd_send, qd_recv, lr_send, lr_recv,
     pg_send, pg_recv, at_send, at_recv, kv_pass, qd_pass,
 ):
@@ -140,19 +140,14 @@
     row_id = lax.broadcasted_iota(jnp.int32, (rows, rows), 0)
     col_id = lax.broadcasted_iota(jnp.int32, (rows, rows), 1)
 
-    one_16 = jnp.ones((rows, wide), jnp.bfloat16)
-
-    def with_ones(block):
-        return jnp.where(lane < pad, one_16, block)
-
-    own_ones = with_ones(own_v)
-    for h in range(heads):
-        s = nt(qm[h], own_k) * factor
-        s = jnp.where(col_id <= row_id, s, masked_score)
-        top = jnp.max(s, axis=1, keepdims=True)
+    for h in range(heads):
+        s = nt(own_k, qm[h]) * factor
+        s = jnp.where(row_id <= col_id, s, masked_score)
+        top = jnp.max(s, axis=0, keepdims=True)
         e = jnp.exp2(s - top)
-        max_s[h] = top
-        acc_a[h] = nn(e.astype(jnp.bfloat16), own_ones)
+        max_r[h] = top
+        sum_r[h] = jnp.sum(e, axis=0, keepdims=True)
+        acc_t[h] = nn(v_ref[h * HD:(h + 1) * HD, :], e.astype(jnp.bfloat16))
 
     def forward(i, carry):
         turn = i - parity + 2
@@ -165,24 +160,26 @@
             pass_on(kv, kv_pass, kv_recv, j).start()
 
         block = kv.at[j]
-        value_ones = with_ones(block[:, high])
+        value_t = block[:, high].T
         for h in range(heads):
-            s = nt(qm[h], block[:, low]) * factor
-            old = max_s[h]
-            top = jnp.maximum(old, jnp.max(s, axis=1, keepdims=True))
+            s = nt(block[:, low], qm[h]) * factor
+            old = max_r[h]
+            top = jnp.maximum(old, jnp.max(s, axis=0, keepdims=True))
             alpha = jnp.exp2(old - top)
             e = jnp.exp2(s - top)
-            max_s[h] = top
-            acc_a[h] = acc_a[h] * alpha + nn(e.astype(jnp.bfloat16), value_ones)
+            max_r[h] = top
+            sum_r[h] = sum_r[h] * alpha + jnp.sum(e, axis=0, keepdims=True)
+            value_h = value_t[pad + h * HD:pad + (h + 1) * HD, :]
+            acc_t[h] = acc_t[h] * alpha + nn(value_h, e.astype(jnp.bfloat16))
         return carry
 
     lax.fori_loop(0, me, forward, 0)
 
-    mixed = jnp.zeros((rows, wide), jnp.float32)
-    for h in range(heads):
-        sum_s[h] = acc_a[h][:, 0:1]
-        mixed = jnp.where(high_mask(h), acc_a[h] * (1.0 / sum_s[h]), mixed)
-    attended = mixed.astype(jnp.bfloat16).astype(jnp.float32)
+    mixed = [jnp.zeros((pad, rows), jnp.float32)]
+    for h in range(heads):
+        mixed.append(acc_t[h] * (1.0 / sum_r[h]))
+    attended_t = jnp.concatenate(mixed, axis=0).astype(jnp.bfloat16).astype(jnp.float32)
+    attended = attended_t.T
     upper = attended[:half, pad:]
     lower = attended[half:, pad:]
     att[hz] = jnp.concatenate([upper, lower], axis=1).astype(jnp.bfloat16)
@@ -221,17 +218,18 @@
     for h in range(heads):
         dom[h] = jnp.where(high_mask(h), own_g, zero_16)
 
-    product = attended * own_g.astype(jnp.float32)
-    stat_lane = lax.broadcasted_iota(jnp.int32, (rows, 128), 1)
-    stats = jnp.zeros((rows, 128), jnp.float32)
-    for h in range(heads):
-        row_dot = jnp.sum(jnp.where(high_mask(h), product, 0.0), axis=1, keepdims=True)
-        log_total = max_s[h] + jnp.log2(sum_s[h])
-        max_s[h] = log_total
-        dot_s[h] = row_dot
-        stats = jnp.where(stat_lane == h, log_total, stats)
-        stats = jnp.where(stat_lane == heads + h, row_dot, stats)
-    lr[me] = stats.T[:stat_rows, :]
+    product = attended_t[pad:, :] * total.astype(jnp.bfloat16).astype(jnp.float32)
+    stat_row = lax.broadcasted_iota(jnp.int32, (128, rows), 0)
+    stats = jnp.zeros((128, rows), jnp.float32)
+    for h in range(heads):
+        row_dot = jnp.sum(product[h * HD:(h + 1) * HD, :], axis=0, keepdims=True)
+        stats = jnp.where(stat_row == h, max_r[h] + jnp.log2(sum_r[h]), stats)
+        stats = jnp.where(stat_row == heads + h, row_dot, stats)
+    lr[me] = stats[:stat_rows, :]
+    columns = stats.T
+    for h in range(heads):
+        max_s[h] = columns[:, h:h + 1]
+        dot_s[h] = columns[:, heads + h:heads + h + 1]
 
     def send_lr(j, carry):
         seq_copy(lr, lr_send, lr_recv, me, j).start()
@@ -392,7 +390,9 @@
         ]
         + [pltpu.VMEM((heads, rows, wide), bf16)] * 4
         + [pltpu.VMEM((heads, rows, wide), f32)] * 3
-        + [pltpu.VMEM((heads, rows, 1), f32)] * 3
+        + [pltpu.VMEM((heads, rows, 1), f32)] * 2
+        + [pltpu.VMEM((heads, HD, rows), f32)]
+        + [pltpu.VMEM((heads, 1, rows), f32)] * 2
         + [dma((m,))]
         + [dma((n,))] * 6
         + [dma((m,))] * 4

time: 38.2 us -> 36.1 us (0.945)
  Pallas kernels: 37.4 us -> 35.2 us
    pallas_call x1, Pallas kernels: 35.5 us -> 33.4 us  [per_device(): pl.pallas_call(functools.partial(kernel, n, m), out_shape=shapes, in_spec...]
where the time goes in v5:
time: 36.1 us; the launch traced here: 35.9 us
  Pallas kernels  35.2 us (98%)
  between operations  0.64 us (2%)
    pallas_call x1, Pallas kernels, per_device(): pl.pallas_call(functools.partial(kernel, n, m), out_shape=shapes, in_spec...  33.4 us
    pallas_call x1, Pallas kernels, per_device(): pl.pallas_call(finish, out_shape=shapes, in_specs=[in_vmem] * 4, out_spec...  1.86 us

profile of v5, /device:TPU:1, one launch (start us, length us, event | category | flops | bytes accessed | tf_op | source)
XLA Modules:
  0.0 35.9 jit_solution(15860220714910982276)
XLA Ops:
  0.6 33.4 %shard_map.84 = (bf16[256,384]{1,0:T(8,128)(2,1)}, bf16[192,256]{1,0:T(8,128)(2,1)}, bf16[192,256]{1,0:T(8,128)(2,1)}, bf16[192,256]{1,0:T(8,128)(2,1)}) custom-call(bf16[192,256]{1,0:T(8,128)(2,1)} %bitcast.6, bf16[192,256]{1,0:T(8,128)(2,1)} %bitcast.7, bf16[192,256]{1,0:T(8,128)(2,1)} %bitcast.8, bf16[768,1536]{1,0:T(8,128)(2,1)} %w_ref.1, ...), custom_call_target="tpu_custom_call" | custom-call | flops 1056964608 | bytes 589824 | tf_op jit(solution)/shard_map/pallas_call | solution.py:377
  34.0 1.9 %shard_map.85 = (bf16[256,384]{1,0:T(8,128)(2,1)}, bf16[192,256]{1,0:T(8,128)(2,1)}, bf16[192,256]{1,0:T(8,128)(2,1)}, bf16[192,256]{1,0:T(8,128)(2,1)}) custom-call(bf16[256,384]{1,0:T(8,128)(2,1)} %get-tuple-element.12.refs_0_, bf16[192,256]{1,0:T(8,128)(2,1)} %get-tuple-element.13.refs_1_, bf16[192,256]{1,0:T(8,128)(2,1)} %get-tuple-element.14.refs_2_, ...), custom_call_target="tpu_custom_call" | custom-call | tf_op jit(solution)/shard_map/pallas_call | solution.py:407
